TPU v7x, 32 devices: a whole 2x2x4 slice. The times are simulated.
32 devices in a mesh: depth: 4 (over x, core), tile: 8 (over z, y).
Axes of the slice: x: 2, y: 2, z: 4, core: 2. Of those that a mesh axis runs over, the one named last changes fastest.
Arguments:
- old_fields: float32 [2, 32, 512, 128], P(None, 'depth', 'tile'), may hold values from -6 to 6
- recv_block: int32 [4, 128], P('depth', 'tile'), may hold values from 0 to 511
- recv_count: int32 [4, 64], P('depth', 'tile'), may hold values from 0 to 2, as said below
- new_block: int32 [4, 128], P('depth', 'tile'), may hold values from 0 to 127
- moments: bfloat16 [4, 128, 4, 128, 128], P('depth', 'tile'), may hold values from -0.0606 to 0.0606, as said below
- new_volume: float32 [4, 1024, 128], P('depth', 'tile'), may hold values from 0.5 to 2
Outputs:
- new_fields: float32 [4, 1024, 2, 128], P('depth', 'tile')
Inputs may be any that keep to these rules, and one draw needn't show every extreme that they name: `recv_count`: the tiles of some quarter of each depth group hold 2 live slots from every source tile. `moments`: component 0 (intersection volumes) is nonnegative.
All inputs are finite; a program needn't handle non-finite values.
Results may differ from a plain program's by a relative error of at most 0.003.
Values may be sent and summed in bfloat16 or wider, within the bound.
A program may use at most 128 MiB of HBM per device.

v0:
```python
import jax
import jax.numpy as jnp
from jax import lax
from jax.sharding import PartitionSpec as P

CAP = 2


def with_halo(array, sides, width):
    for axis, dim in sides:
        size, length = (lax.axis_size(axis), array.shape[dim])
        up = [(i, (i + 1) % size) for i in range(size - 1)]
        down = [(j, i) for i, j in up]
        last = lax.slice_in_dim(array, length - width, length, axis=dim)
        initial = lax.slice_in_dim(array, 0, width, axis=dim)
        before = lax.ppermute(last, axis, up)
        after = lax.ppermute(initial, axis, down)
        array = jnp.concatenate([before, array, after], axis=dim)
    return array


def minmod(left_value, right_value):
    return (
        0.5
        * (jnp.sign(left_value) + jnp.sign(right_value))
        * jnp.minimum(jnp.abs(left_value), jnp.abs(right_value))
    )


def limited(centre, upper_side, lower_side):
    central = 0.5 * (upper_side - lower_side)
    return minmod(central, minmod(2.0 * (centre - lower_side), 2.0 * (upper_side - centre)))


def interior(offset, length, total):
    position = offset + jnp.arange(length, dtype=jnp.int32)
    return ((position > 0) & (position < total - 1)).astype(jnp.float32)


def per_device(old_fields, recv_block, recv_count, new_block, moments, new_volume):
    padded = with_halo(old_fields, (("depth", 1), ("tile", 2)), 1)
    centre = padded[:, 1:-1, 1:-1, :]
    layers = centre.shape[1]
    lateral = centre.shape[2]
    width_x = centre.shape[3]
    depth_keep = interior(lax.axis_index("depth") * layers, layers, layers * lax.axis_size("depth"))
    lateral_keep = interior(
        lax.axis_index("tile") * lateral, lateral, lateral * lax.axis_size("tile")
    )
    x_keep = interior(0, width_x, width_x)
    slope_depth = (
        limited(centre, padded[:, 2:, 1:-1, :], padded[:, :-2, 1:-1, :])
        * depth_keep[None, :, None, None]
    )
    slope_lateral = (
        limited(centre, padded[:, 1:-1, 2:, :], padded[:, 1:-1, :-2, :])
        * lateral_keep[None, None, :, None]
    )
    x_padded = jnp.pad(centre, ((0, 0), (0, 0), (0, 0), (1, 1)))
    slope_x = limited(centre, x_padded[..., 2:], x_padded[..., :-2]) * x_keep
    stacked = jnp.stack([centre, slope_depth, slope_lateral, slope_x], 0).transpose(2, 3, 0, 1, 4)
    blocks = stacked.reshape(layers * lateral, 8, width_x).astype(jnp.bfloat16)
    block_count = layers * lateral
    slot_count = recv_block.shape[1]
    source = jnp.arange(slot_count, dtype=jnp.int32) // CAP
    gathered = lax.all_gather(blocks, "tile", axis=0, tiled=True)
    fetched = gathered[source * block_count + recv_block[0]]
    alive_mask = (jnp.arange(slot_count, dtype=jnp.int32) % CAP < recv_count[0][source]).astype(
        jnp.float32
    )
    contribution = jnp.einsum(
        "jcno,jcfo->jfn",
        moments[0],
        fetched.reshape(slot_count, 4, 2, width_x),
        preferred_element_type=jnp.float32,
    )
    contribution = contribution * alive_mask[:, None, None]
    new_count = new_volume.shape[1]
    one_hot = (new_block[0][None, :] == jnp.arange(new_count, dtype=jnp.int32)[:, None]).astype(
        jnp.float32
    )
    summed = jnp.dot(
        one_hot, contribution.reshape(slot_count, 2 * width_x), precision=lax.Precision.HIGHEST
    )
    result = summed.reshape(new_count, 2, width_x) / new_volume[0][:, None, :]
    return result[None]


def solution(mesh):
    placed = (
        P(None, "depth", "tile", None),
        P("depth", "tile"),
        P("depth", "tile"),
        P("depth", "tile"),
        P("depth", "tile", None, None, None),
        P("depth", "tile", None),
    )
    return jax.shard_map(
        per_device,
        mesh=mesh,
        in_specs=placed,
        out_specs=P("depth", "tile", None, None),
        check_vma=False,
    )
```

profile of v0, /device:TPU:0, one launch (start us, length us, event | category | flops | bytes accessed | tf_op | source)
XLA Modules:
  0.0 171.6 jit_solution(12616896355087981375)
XLA Ops:
  6.5 0.0 copy-start
  6.5 0.0 copy-start.2
  6.5 0.0 all-gather.2.cloned.1.call-start
  6.5 1.0 fusion.26
  7.6 2.4 %collective-permute-start.1 = (f32[2,1,64,128]{3,2,1,0:T(8,128)S(1)}, f32[2,1,64,128]{3,2,1,0:T(8,128)S(1)}, u32[]{:S(2)}, u32[]{:S(2)}) collective-permute-start(f32[2,1,64,128]{3,2,1,0:T(8,128)S(1)} %get-tuple-element.12), channel_id=1, source_target_pairs={{0,8},{8,16},{16,24},{1,9},{9,17},{17,25},{2,10},{10,18},{18,26},{... | collective-permute-start | bytes 196616 | tf_op jit(solution)/shard_map/ppermute | solution.py:16
  9.9 1.3 collective-permute-start
  11.3 0.0 collective-permute-done.1
  11.3 3.9 %collective-permute-done = f32[2,1,64,128]{3,2,1,0:T(8,128)S(1)} collective-permute-done((f32[2,1,64,128]{3,2,1,0:T(8,128)S(1)}, f32[2,1,64,128]{3,2,1,0:T(8,128)S(1)}, u32[]{:S(2)}, u32[]{:S(2)}) %collective-permute-start) | collective-permute-done | bytes 65568 | tf_op jit(solution)/shard_map/ppermute | solution.py:17
  15.2 4.1 %convert_bitcast_fusion = (bf16[1,2,8,64,128]{4,3,2,1,0:T(8,128)(2,1)S(1)}, f32[2,10,64,128]{3,2,1,0:T(8,128)S(1)}, bf16[1,2,8,64,128]{4,3,2,1,0:T(8,128)(2,1)S(1)}, bf16[1,2,8,64,128]{4,3,2,1,0:T(8,128)(2,1)S(1)}) fusion(f32[2,8,64,128]{3,2,1,0:T(8,128)} %param.6, f32[2,10,64,128]{3,2,1,0:T(8,128)S(1)} %constant_dynamic-update-slice_fusion.2, ...), kind=kLoop, calls=%fused_computation.24 | loop fusion | flops 6684672 | bytes 1967104 | tf_op jit(solution)/shard_map/stack | solution.py:61
  19.3 1.3 collective-permute-start.2
  20.6 4.5 %collective-permute-start.3 = (f32[2,10,1,128]{3,2,1,0:T(1,128)S(1)}, f32[2,10,1,128]{3,2,1,0:T(1,128)S(1)}, u32[]{:S(2)}, u32[]{:S(2)}) collective-permute-start(f32[2,10,1,128]{3,2,1,0:T(1,128)S(1)} %get-tuple-element.6), channel_id=1, source_target_pairs={{0,1},{1,2},{2,3},{3,4},{4,5},{5,6},{6,7},{8,9},{9,10},{10,11},{11... | collective-permute-start | bytes 30728 | tf_op jit(solution)/shard_map/ppermute | solution.py:16
  25.2 0.0 collective-permute-done.2
  25.2 1.3 collective-permute-done.3
  26.5 0.0 copy-done.2
  26.6 0.9 fusion.16
  27.5 0.1 maximum_bitcast_fusion
  27.6 0.0 copy-start.1
  27.6 0.0 copy-start.4
  27.6 2.1 %copy.12 = bf16[8,64,4,2,128]{4,3,2,1,0:T(2,128)(2,1)} copy(bf16[8,64,4,2,128]{4,1,0,3,2:T(8,128)(2,1)S(1)} %maximum_bitcast_fusion) | data formatting | bytes 2097152 | tf_op jit(solution)/shard_map/convert_element_type | solution.py:62
  29.8 0.0 copy-start.3
  29.8 0.0 copy-start.5
  29.8 0.0 all-gather.2.cloned.1.call-update
  29.8 0.0 copy-done.1
  29.8 0.7 gather_fusion.1
  30.5 0.0 copy-done.4
  30.5 128.5 %all-gather.2.cloned.1.call-done = bf16[4096,8,128]{2,1,0:T(8,128)(2,1)} async-done(((bf16[512,8,128]{2,1,0:T(8,128)(2,1)}), bf16[4096,8,128]{2,1,0:T(8,128)(2,1)}) %all-gather.2.cloned.1.call-update) | async-done | bytes 8388624 | tf_op jit(solution)/shard_map/all_gather | solution.py:66
  159.0 4.0 %gather_fusion = bf16[16,8,128]{2,1,0:T(8,128)(2,1)S(1)} fusion(bf16[4096,8,128]{2,1,0:T(8,128)(2,1)} %all-gather.2.cloned.1.call-done, s32[1024]{0:T(1024)S(1)} %pad_clamp_fusion.1), kind=kCustom, calls=%fused_computation | custom fusion | bytes 65600 | tf_op jit(solution)/shard_map/gather | solution.py:67
  163.0 0.0 copy-done
  163.0 0.7 fusion.6
  163.6 0.0 copy-done.3
  163.7 0.0 copy-done.5
  163.7 0.3 fusion.2
  164.0 0.8 copy.14
  (11 shorter events, 0.1 us)
Async XLA Ops:
  6.5 156.5 %copy-start = (bf16[1,16,4,128,128]{4,3,2,1,0:T(8,128)(2,1)S(1)}, bf16[1,16,4,128,128]{4,3,2,1,0:T(8,128)(2,1)}, u32[]{:S(2)}) copy-start(bf16[1,16,4,128,128]{4,3,2,1,0:T(8,128)(2,1)} %param.10) | copy-start | bytes 6291460
  6.5 20.0 %copy-start.2 = (f32[2,8,64,128]{3,2,1,0:T(8,128)S(1)}, f32[2,8,64,128]{3,2,1,0:T(8,128)}, u32[]{:S(2)}) copy-start(f32[2,8,64,128]{3,2,1,0:T(8,128)} %param.6) | copy-start | bytes 1572868
  6.5 152.5 %all-gather.2.cloned.1.call-start = ((), (), s32[]{:S(2)}) async-start(), calls=%async_computation | async-start | bytes 9437184 | tf_op jit(solution)/shard_map/all_gather | solution.py:66
  7.6 3.7 %collective-permute-start.1 = (f32[2,1,64,128]{3,2,1,0:T(8,128)S(1)}, f32[2,1,64,128]{3,2,1,0:T(8,128)S(1)}, u32[]{:S(2)}, u32[]{:S(2)}) collective-permute-start(f32[2,1,64,128]{3,2,1,0:T(8,128)S(1)} %get-tuple-element.12), channel_id=1, source_target_pairs={{0,8},{8,16},{16,24},{1,9},{9,17},{17,25},{2,10},{10,18},{18,26},{... | collective-permute-start | bytes 196616 | tf_op jit(solution)/shard_map/ppermute | solution.py:16
  9.9 5.3 %collective-permute-start = (f32[2,1,64,128]{3,2,1,0:T(8,128)S(1)}, f32[2,1,64,128]{3,2,1,0:T(8,128)S(1)}, u32[]{:S(2)}, u32[]{:S(2)}) collective-permute-start(f32[2,1,64,128]{3,2,1,0:T(8,128)S(1)} %get-tuple-element.11), channel_id=1, source_target_pairs={{8,0},{16,8},{24,16},{9,1},{17,9},{25,17},{10,2},{18,10},{26,18},{... | collective-permute-start | bytes 196616 | tf_op jit(solution)/shard_map/ppermute | solution.py:17
  19.3 5.9 %collective-permute-start.2 = (f32[2,10,1,128]{3,2,1,0:T(1,128)S(1)}, f32[2,10,1,128]{3,2,1,0:T(1,128)S(1)}, u32[]{:S(2)}, u32[]{:S(2)}) collective-permute-start(f32[2,10,1,128]{3,2,1,0:T(1,128)S(1)} %get-tuple-element.5), channel_id=1, source_target_pairs={{1,0},{2,1},{3,2},{4,3},{5,4},{6,5},{7,6},{9,8},{10,9},{11,10},{12... | collective-permute-start | bytes 30728 | tf_op jit(solution)/shard_map/ppermute | solution.py:17
  20.6 5.9 %collective-permute-start.3 = (f32[2,10,1,128]{3,2,1,0:T(1,128)S(1)}, f32[2,10,1,128]{3,2,1,0:T(1,128)S(1)}, u32[]{:S(2)}, u32[]{:S(2)}) collective-permute-start(f32[2,10,1,128]{3,2,1,0:T(1,128)S(1)} %get-tuple-element.6), channel_id=1, source_target_pairs={{0,1},{1,2},{2,3},{3,4},{4,5},{5,6},{6,7},{8,9},{9,10},{10,11},{11... | collective-permute-start | bytes 30728 | tf_op jit(solution)/shard_map/ppermute | solution.py:16
  27.6 2.2 %copy-start.1 = (s32[1,8]{1,0:T(1,128)S(1)}, s32[1,8]{1,0:T(1,128)}, u32[]{:S(2)}) copy-start(s32[1,8]{1,0:T(1,128)} %param.8) | copy-start | bytes 100
  27.6 2.9 %copy-start.4 = (s32[1,16]{1,0:T(1,128)S(1)}, s32[1,16]{1,0:T(1,128)}, u32[]{:S(2)}) copy-start(s32[1,16]{1,0:T(1,128)} %param.7) | copy-start | bytes 196
  29.8 133.9 %copy-start.3 = (f32[1,128,128]{2,1,0:T(8,128)S(1)}, f32[1,128,128]{2,1,0:T(8,128)}, u32[]{:S(2)}) copy-start(f32[1,128,128]{2,1,0:T(8,128)} %param.11) | copy-start | bytes 196612
  29.8 133.9 %copy-start.5 = (s32[1,16]{1,0:T(1,128)S(1)}, s32[1,16]{1,0:T(1,128)}, u32[]{:S(2)}) copy-start(s32[1,16]{1,0:T(1,128)} %param.9) | copy-start | bytes 196
Sparse Core Ops, SparseCore 0:
  29.9 129.0 all-gather.1
where the time goes:
time: 172 us
  waiting for transfers between devices  134 us (78%)
  between operations  13.6 us (8%)
  starting transfers between devices  9.49 us (6%)
  local copies, waits for them, and re-layouts  8.61 us (5%)
  other arithmetic  5.17 us (3%)
    all_gather x1, waiting for transfers between devices, per_device(): gathered = lax.all_gather(blocks, 'tile', axis=0, tiled=True)  128 us
    ppermute x2, starting transfers between devices, with_halo(): before = lax.ppermute(last, axis, up)  6.91 us
    another operation x2, other arithmetic, per_device(): jnp.stack([centre, slope_depth, slope_lateral, slope_x], 0)  4.98 us
    gather x1, local copies, waits for them, and re-layouts, per_device(): fetched = gathered[source * block_count + recv_block[0]]  3.96 us
    ppermute x2, waiting for transfers between devices, with_halo(): after = lax.ppermute(initial, axis, down)  3.9 us
  transfers between devices with their start and end apart: 5, of which 3 were waited for; matrix products, arithmetic and copies ran while one was open for 0% of the time, Pallas kernels for 0%

commit v1 on v0

v1 whole, which is shorter than its diff:
```python
import functools

import jax
import jax.numpy as jnp
from jax import lax
from jax.experimental import pallas as pl
from jax.experimental.pallas import tpu as pltpu
from jax.sharding import PartitionSpec as P

CAP = 2
ROWS = 8
EDGE = 8
MESH = pl.DeviceIdType.MESH


def limited(centre, upper_side, lower_side):
    central = 0.5 * (upper_side - lower_side)
    left = 2.0 * (centre - lower_side)
    right = 2.0 * (upper_side - centre)
    low = jnp.minimum(central, jnp.minimum(left, right))
    high = jnp.maximum(central, jnp.maximum(left, right))
    return jnp.maximum(low, 0.0) + jnp.minimum(high, 0.0)


def kernel(
    n_depth, n_tile,
    fields, blocks, counts, targets, moments,
    out,
    pad, asked, count_s, target_s, weights, sending, states, partial,
    local_sem, ask_send, ask_recv, halo_send, halo_recv, state_send, state_recv,
):
    layers, lateral, width = fields.shape[1:]
    slots = blocks.shape[1]
    depth = lax.axis_index("depth")
    me = lax.axis_index("tile")

    load_fields = pltpu.make_async_copy(
        fields, pad.at[:, pl.ds(1, layers), pl.ds(EDGE, lateral), :], local_sem.at[0]
    )
    load_asked = pltpu.make_async_copy(blocks, asked.at[me], local_sem.at[1])
    load_count = pltpu.make_async_copy(counts, count_s, local_sem.at[2])
    load_target = pltpu.make_async_copy(targets, target_s, local_sem.at[3])
    load_weights = pltpu.make_async_copy(moments, weights, local_sem.at[4])
    load_asked.start()
    load_fields.start()
    load_count.start()
    load_target.start()
    load_weights.start()

    barrier = pltpu.get_barrier_semaphore()

    def greet(step, carry):
        peer = lax.rem(me + step, n_tile)
        pl.semaphore_signal(barrier, inc=1, device_id=(depth, peer), device_id_type=MESH)
        return carry

    lax.fori_loop(1, n_tile, greet, 0)

    @pl.when(depth > 0)
    def _():
        pl.semaphore_signal(barrier, inc=1, device_id=(depth - 1, me), device_id_type=MESH)

    @pl.when(depth < n_depth - 1)
    def _():
        pl.semaphore_signal(barrier, inc=1, device_id=(depth + 1, me), device_id_type=MESH)

    edges = (depth > 0).astype(jnp.int32) + (depth < n_depth - 1).astype(jnp.int32)
    pl.semaphore_wait(barrier, n_tile - 1 + edges)

    def ask(peer, slot):
        return pltpu.make_async_remote_copy(
            src_ref=blocks, dst_ref=asked.at[slot],
            send_sem=ask_send.at[peer], recv_sem=ask_recv.at[slot],
            device_id=(depth, peer), device_id_type=MESH,
        )

    def halo(which, source, target, device):
        return pltpu.make_async_remote_copy(
            src_ref=source, dst_ref=target,
            send_sem=halo_send.at[which], recv_sem=halo_recv.at[which],
            device_id=device, device_id_type=MESH,
        )

    def answer(peer, slot):
        return pltpu.make_async_remote_copy(
            src_ref=sending.at[peer], dst_ref=states.at[slot],
            send_sem=state_send.at[peer], recv_sem=state_recv.at[slot],
            device_id=(depth, peer), device_id_type=MESH,
        )

    inner = pl.ds(EDGE, lateral)
    body = pl.ds(1, layers)
    halos = (
        (depth < n_depth - 1, depth > 0, halo(
            0, fields.at[:, layers - 1], pad.at[:, 0, inner, :],
            (lax.rem(depth + 1, n_depth), me))),
        (depth > 0, depth < n_depth - 1, halo(
            1, fields.at[:, 0], pad.at[:, layers + 1, inner, :],
            (lax.rem(depth + n_depth - 1, n_depth), me))),
        (me < n_tile - 1, me > 0, halo(
            2, fields.at[:, :, pl.ds(lateral - EDGE, EDGE), :], pad.at[:, body, pl.ds(0, EDGE), :],
            (depth, lax.rem(me + 1, n_tile)))),
        (me > 0, me < n_tile - 1, halo(
            3, fields.at[:, :, pl.ds(0, EDGE), :], pad.at[:, body, pl.ds(EDGE + lateral, EDGE), :],
            (depth, lax.rem(me + n_tile - 1, n_tile)))),
    )

    def ask_step(step, carry):
        ask(lax.rem(me + step, n_tile), me).start()
        return carry

    lax.fori_loop(1, n_tile, ask_step, 0)
    for sends, _, copy in halos:
        pl.when(sends)(copy.start)

    load_count.wait()
    load_target.wait()
    columns = slots * ROWS
    lane = lax.broadcasted_iota(jnp.int32, (2 * EDGE, columns), 1)
    new_of = jnp.zeros((2 * EDGE, columns), jnp.int32)
    live = jnp.zeros((2 * EDGE, columns), jnp.int32)
    for j in range(slots):
        new_of = jnp.where(lane // ROWS == j, target_s[0, j], new_of)
    for s in range(n_tile):
        live = jnp.where(lane // (ROWS * CAP) == s, count_s[0, s], live)
    row_of = jnp.where(lane // ROWS % CAP < live, 2 * new_of + lane % 2, -1)
    row_of = jnp.broadcast_to(row_of[:1], (out.shape[0], columns))
    line = lax.broadcasted_iota(jnp.int32, (out.shape[0], columns), 0)
    one_hot = jnp.where(row_of == line, 1.0, 0.0).astype(jnp.bfloat16)

    load_fields.wait()

    @pl.when(depth == 0)
    def _():
        pad[:, 0, inner, :] = pad[:, 1, inner, :]

    @pl.when(depth == n_depth - 1)
    def _():
        pad[:, layers + 1, inner, :] = pad[:, layers, inner, :]

    @pl.when(me == 0)
    def _():
        pad[:, body, pl.ds(EDGE - 1, 1), :] = pad[:, body, pl.ds(EDGE, 1), :]

    @pl.when(me == n_tile - 1)
    def _():
        pad[:, body, pl.ds(EDGE + lateral, 1), :] = pad[:, body, pl.ds(EDGE + lateral - 1, 1), :]

    for _, receives, copy in halos:
        pl.when(receives)(copy.wait_recv)
    load_asked.wait()

    x = lax.broadcasted_iota(jnp.int32, (2, width), 1)
    x_inside = (x > 0) & (x < width - 1)

    def state_of(peer):
        pieces = []
        for c in range(CAP):
            number = asked[peer, 0, CAP * me + c]
            z = lax.div(number, lateral) + 1
            y = lax.rem(number, lateral) + EDGE
            centre, below, above, before, after = (
                pad[:, z + dz, pl.ds(y + dy, 1), :].reshape(2, width)
                for dz, dy in ((0, 0), (-1, 0), (1, 0), (0, -1), (0, 1))
            )
            along_x = limited(centre, pltpu.roll(centre, width - 1, 1), pltpu.roll(centre, 1, 1))
            pieces += [
                centre,
                limited(centre, above, below),
                limited(centre, after, before),
                jnp.where(x_inside, along_x, 0.0),
            ]
        return jnp.concatenate(pieces, axis=0).astype(jnp.bfloat16)

    def answer_step(step, carry):
        peer = lax.rem(me + step, n_tile)
        ask(peer, peer).wait_recv()
        sending[peer] = state_of(peer)
        answer(peer, me).start()
        return carry

    lax.fori_loop(1, n_tile, answer_step, 0)
    states[me] = state_of(me)

    load_weights.wait()
    kind = lax.broadcasted_iota(jnp.int32, (CAP * ROWS, width), 0) // 2

    def sum_step(step, carry):
        source = lax.rem(me + step, n_tile)

        @pl.when(step > 0)
        def _():
            answer(source, source).wait_recv()

        state = states[source]
        zero = jnp.zeros_like(state)
        left = jnp.concatenate(
            [jnp.where(kind == i, state, zero) for i in range(CAP * 4)], axis=1
        )
        right = jnp.concatenate(
            [weights[0, CAP * source + i // 4, i % 4] for i in range(CAP * 4)], axis=1
        )
        first = pl.multiple_of(source * (CAP * ROWS), CAP * ROWS)
        partial[pl.ds(first, CAP * ROWS), :] = lax.dot_general(
            left, right, (((1,), (1,)), ((), ())), preferred_element_type=jnp.float32
        )
        return carry

    lax.fori_loop(0, n_tile, sum_step, 0)

    total = partial[...]
    high = total.astype(jnp.bfloat16)
    low = (total - high.astype(jnp.float32)).astype(jnp.bfloat16)
    out[...] = jnp.dot(one_hot, high, preferred_element_type=jnp.float32) + jnp.dot(
        one_hot, low, preferred_element_type=jnp.float32
    )

    for sends, _, copy in halos:
        pl.when(sends)(copy.wait_send)

    def finish(step, carry):
        peer = lax.rem(me + step, n_tile)
        ask(peer, me).wait_send()
        answer(peer, me).wait_send()
        return carry

    lax.fori_loop(1, n_tile, finish, 0)


def per_device(n_depth, n_tile, old_fields, recv_block, recv_count, new_block, moments, new_volume):
    fields, layers, lateral, width = old_fields.shape
    slots = recv_block.shape[1]
    new_count = new_volume.shape[1]
    anywhere = pl.BlockSpec(memory_space=pl.ANY)
    summed = pl.pallas_call(
        functools.partial(kernel, n_depth, n_tile),
        out_shape=jax.ShapeDtypeStruct((2 * new_count, width), jnp.float32),
        in_specs=[anywhere] * 5,
        out_specs=pl.BlockSpec(memory_space=pltpu.VMEM),
        scratch_shapes=[
            pltpu.VMEM((fields, layers + 2, lateral + 2 * EDGE, width), jnp.float32),
            pltpu.SMEM((n_tile, 1, slots), jnp.int32),
            pltpu.SMEM(recv_count.shape, jnp.int32),
            pltpu.SMEM(new_block.shape, jnp.int32),
            pltpu.VMEM(moments.shape, jnp.bfloat16),
            pltpu.VMEM((n_tile, CAP * ROWS, width), jnp.bfloat16),
            pltpu.VMEM((n_tile, CAP * ROWS, width), jnp.bfloat16),
            pltpu.VMEM((slots * ROWS, width), jnp.float32),
            pltpu.SemaphoreType.DMA((5,)),
            pltpu.SemaphoreType.DMA((n_tile,)),
            pltpu.SemaphoreType.DMA((n_tile,)),
            pltpu.SemaphoreType.DMA((4,)),
            pltpu.SemaphoreType.DMA((4,)),
            pltpu.SemaphoreType.DMA((n_tile,)),
            pltpu.SemaphoreType.DMA((n_tile,)),
        ],
        compiler_params=pltpu.CompilerParams(
            collective_id=0, has_side_effects=True, vmem_limit_bytes=63 * 2**20
        ),
    )(old_fields, recv_block, recv_count, new_block, moments)
    result = summed.reshape(new_count, 2, width) / new_volume[0][:, None, :]
    return result[None]


def solution(mesh):
    placed = (
        P(None, "depth", "tile", None),
        P("depth", "tile"),
        P("depth", "tile"),
        P("depth", "tile"),
        P("depth", "tile", None, None, None),
        P("depth", "tile", None),
    )
    return jax.shard_map(
        functools.partial(per_device, mesh.shape["depth"], mesh.shape["tile"]),
        mesh=mesh,
        in_specs=placed,
        out_specs=P("depth", "tile", None, None),
        check_vma=False,
    )
```

time: 172 us -> 18.3 us (0.11)
  waiting for transfers between devices: 134 us -> 0 us
  Pallas kernels: 0 us -> 16.5 us
  between operations: 13.6 us -> 0.02 us
  starting transfers between devices: 9.49 us -> 0 us
  local copies, waits for them, and re-layouts: 8.61 us -> 0.01 us
  other arithmetic: 5.17 us -> 1.63 us
    all_gather x1 -> x0, waiting for transfers between devices: 128 us -> none  [per_device(): gathered = lax.all_gather(blocks, 'tile', axis=0, tiled=True)]
    pallas_call x0 -> x1, Pallas kernels: none -> 16.5 us  [per_device(): pl.pallas_call(functools.partial(kernel, n_depth, n_tile), out_shape=jax....]
    ppermute x4 -> x0, starting transfers between devices: 9.49 us -> none  [the longest x2 6.91 us: with_halo(): before = lax.ppermute(last, axis, up)]
    ppermute x4 -> x0, waiting for transfers between devices: 5.24 us -> none  [the longest x2 3.9 us: with_halo(): after = lax.ppermute(initial, axis, down)]
    another operation x2 -> x0, other arithmetic: 4.98 us -> none  [per_device(): jnp.stack([centre, slope_depth, slope_lateral, slope_x], 0)]
    gather x2 -> x0, local copies, waits for them, and re-layouts: 4.61 us -> none  [the longest x1 3.96 us: per_device(): fetched = gathered[source * block_count + recv_block[0]]]
    convert_element_type x1 -> x0, local copies, waits for them, and re-layouts: 2.14 us -> none  [per_device(): blocks = stacked.reshape(layers * lateral, 8, width_x).astype(jnp.bfloat16)]
  transfers between devices with their start and end apart: 5 -> 0, of which waited for: 3 -> 0; matrix products, arithmetic and copies ran while one was open for 0% -> 0% of each run, Pallas kernels for 0% -> 0%
where the time goes in v1:
time: 18.3 us; the launch traced here: 18.2 us
  Pallas kernels  16.5 us (90%)
  other arithmetic  1.63 us (9%)
    pallas_call x1, Pallas kernels, per_device(): pl.pallas_call(functools.partial(kernel, n_depth, n_tile), out_shape=jax....  16.5 us
    div x1, other arithmetic, per_device(): result = summed.reshape(new_count, 2, width) / new_volume[0][:, None, :]  1.63 us

profile of v1, /device:TPU:0, one launch (start us, length us, event | category | flops | bytes accessed | tf_op | source)
XLA Modules:
  0.0 18.2 jit_solution(7676032462612636674)
XLA Ops:
  0.0 0.0 copy-start
  0.0 16.5 %shard_map.64 = f32[256,128]{1,0:T(8,128)} custom-call(f32[2,8,64,128]{3,2,1,0:T(8,128)} %fields.1, s32[1,16]{1,0:T(1,128)} %blocks.1, s32[1,8]{1,0:T(1,128)} %counts.1, s32[1,16]{1,0:T(1,128)} %targets.1, bf16[1,16,4,128,128]{4,3,2,1,0:T(8,128)(2,1)} %moments.1), custom_call_target="tpu_custom_call" | custom-call | tf_op jit(solution)/shard_map/pallas_call | solution.py:235
  16.5 0.0 copy-done
  16.6 1.6 %broadcast_divide_fusion = f32[1,128,2,128]{3,2,1,0:T(2,128)} fusion(f32[1,128,2,128]{3,2,1,0:T(2,128)} %bitcast.2, f32[128,128]{1,0:T(8,128)S(1)} %bitcast.3), kind=kLoop, calls=%fused_computation | loop fusion | flops 32768 | bytes 327680 | tf_op jit(solution)/shard_map/div | solution.py:261
Async XLA Ops:
  0.0 16.5 %copy-start = (f32[1,128,128]{2,1,0:T(8,128)S(1)}, f32[1,128,128]{2,1,0:T(8,128)}, u32[]{:S(2)}) copy-start(f32[1,128,128]{2,1,0:T(8,128)} %param.11) | copy-start | bytes 196612

commit v2 on v1

v2 whole, which is shorter than its diff:
```python
import functools

import jax
import jax.numpy as jnp
from jax import lax
from jax.experimental import pallas as pl
from jax.experimental.pallas import tpu as pltpu
from jax.sharding import PartitionSpec as P

CAP = 2
ROWS = 8
EDGE = 8
MESH = pl.DeviceIdType.MESH


def limited(centre, upper_side, lower_side):
    central = 0.5 * (upper_side - lower_side)
    left = 2.0 * (centre - lower_side)
    right = 2.0 * (upper_side - centre)
    low = jnp.minimum(central, jnp.minimum(left, right))
    high = jnp.maximum(central, jnp.maximum(left, right))
    return jnp.maximum(low, 0.0) + jnp.minimum(high, 0.0)


def against(left, right):
    return lax.dot_general(
        left, right, (((1,), (1,)), ((), ())), preferred_element_type=jnp.float32
    )


def kernel(
    n_depth, n_tile,
    fields, blocks, counts, targets, moments, volume,
    out,
    pad, ends, beside, asked, weights, count_s, target_s, volume_v, volume_2, partial, sending, states,
    local_sem, ask_send, ask_recv, halo_send, halo_recv, state_send, state_recv,
):
    layers, lateral, width = fields.shape[1:]
    slots = blocks.shape[1]
    depth = lax.axis_index("depth")
    me = lax.axis_index("tile")
    inner = pl.ds(EDGE, lateral)
    body = pl.ds(1, layers)

    load_fields = pltpu.make_async_copy(
        fields, pad.at[:, pl.ds(1, layers), pl.ds(EDGE, lateral), :], local_sem.at[0]
    )
    load_asked = pltpu.make_async_copy(blocks, asked.at[me], local_sem.at[1])
    load_count = pltpu.make_async_copy(counts, count_s, local_sem.at[3])
    load_target = pltpu.make_async_copy(targets, target_s, local_sem.at[4])
    load_volume = pltpu.make_async_copy(volume, volume_v, local_sem.at[5])
    load_weights = pltpu.make_async_copy(moments, weights, local_sem.at[2])
    def other(step):
        return step + (step >= me).astype(jnp.int32)

    barrier = pltpu.get_barrier_semaphore()

    def greet(step, carry):
        peer = other(step)
        pl.semaphore_signal(barrier, inc=1, device_id=(depth, peer), device_id_type=MESH)
        return carry

    lax.fori_loop(0, n_tile - 1, greet, 0)

    @pl.when(depth > 0)
    def _():
        pl.semaphore_signal(barrier, inc=1, device_id=(depth - 1, me), device_id_type=MESH)

    @pl.when(depth < n_depth - 1)
    def _():
        pl.semaphore_signal(barrier, inc=1, device_id=(depth + 1, me), device_id_type=MESH)

    load_asked.start()
    load_fields.start()
    load_weights.start()
    load_count.start()
    load_target.start()
    load_volume.start()

    load_fields.wait()
    ends[0] = pad[:, body, EDGE, :]
    ends[1] = pad[:, body, EDGE + lateral - 1, :]

    edges = (depth > 0).astype(jnp.int32) + (depth < n_depth - 1).astype(jnp.int32)
    pl.semaphore_wait(barrier, n_tile - 1 + edges)

    def ask(peer, slot):
        return pltpu.make_async_remote_copy(
            src_ref=blocks, dst_ref=asked.at[slot],
            send_sem=ask_send.at[peer], recv_sem=ask_recv.at[slot],
            device_id=(depth, peer), device_id_type=MESH,
        )

    def halo(which, source, target, device):
        return pltpu.make_async_remote_copy(
            src_ref=source, dst_ref=target,
            send_sem=halo_send.at[which], recv_sem=halo_recv.at[which],
            device_id=device, device_id_type=MESH,
        )

    def answer(peer, slot):
        return pltpu.make_async_remote_copy(
            src_ref=sending.at[peer], dst_ref=states.at[slot],
            send_sem=state_send.at[peer], recv_sem=state_recv.at[slot],
            device_id=(depth, peer), device_id_type=MESH,
        )

    halos = (
        (depth < n_depth - 1, depth > 0, halo(
            0, fields.at[:, layers - 1], pad.at[:, 0, inner, :],
            (lax.rem(depth + 1, n_depth), me))),
        (depth > 0, depth < n_depth - 1, halo(
            1, fields.at[:, 0], pad.at[:, layers + 1, inner, :],
            (lax.rem(depth + n_depth - 1, n_depth), me))),
        (me < n_tile - 1, me > 0, halo(
            2, ends.at[1], beside.at[0],
            (depth, lax.rem(me + 1, n_tile)))),
        (me > 0, me < n_tile - 1, halo(
            3, ends.at[0], beside.at[1],
            (depth, lax.rem(me + n_tile - 1, n_tile)))),
    )

    def ask_step(step, carry):
        ask(other(n_tile - 2 - step), me).start()
        return carry

    lax.fori_loop(0, n_tile - 1, ask_step, 0)
    for sends, _, copy in halos:
        pl.when(sends)(copy.start)

    load_count.wait()
    load_target.wait()
    load_volume.wait()
    slots = blocks.shape[1]
    half = volume.shape[1]
    volume_2[pl.ds(0, half, stride=2), :] = volume_v[0]
    volume_2[pl.ds(1, half, stride=2), :] = volume_v[0]
    columns = slots * ROWS
    lane = lax.broadcasted_iota(jnp.int32, (2 * EDGE, columns), 1)
    new_of = jnp.zeros((2 * EDGE, columns), jnp.int32)
    live = jnp.zeros((2 * EDGE, columns), jnp.int32)
    for j in range(slots):
        new_of = jnp.where(lane // ROWS == j, target_s[0, j], new_of)
    for s in range(n_tile):
        live = jnp.where(lane // (ROWS * CAP) == s, count_s[0, s], live)
    row_of = jnp.where(lane // ROWS % CAP < live, 2 * new_of + lane % 2, -1)
    row_of = jnp.broadcast_to(row_of[:1], (out.shape[0], columns))
    line = lax.broadcasted_iota(jnp.int32, (out.shape[0], columns), 0)
    one_hot = jnp.where(row_of == line, 1.0, 0.0).astype(jnp.bfloat16)

    @pl.when(depth == 0)
    def _():
        pad[:, 0, inner, :] = pad[:, 1, inner, :]

    @pl.when(depth == n_depth - 1)
    def _():
        pad[:, layers + 1, inner, :] = pad[:, layers, inner, :]

    @pl.when(me == 0)
    def _():
        pad[:, body, EDGE - 1, :] = ends[0]

    @pl.when(me == n_tile - 1)
    def _():
        pad[:, body, EDGE + lateral, :] = ends[1]

    @pl.when(me > 0)
    def _():
        halos[2][2].wait_recv()
        pad[:, body, EDGE - 1, :] = beside[0]

    @pl.when(me < n_tile - 1)
    def _():
        halos[3][2].wait_recv()
        pad[:, body, EDGE + lateral, :] = beside[1]

    load_asked.wait()
    for _, receives, copy in halos[:2]:
        pl.when(receives)(copy.wait_recv)

    x = lax.broadcasted_iota(jnp.int32, (ROWS, width), 1)
    x_inside = (x > 0) & (x < width - 1)
    part = lax.broadcasted_iota(jnp.int32, (ROWS, width), 0)
    of_field = part % 2 == 0
    part = part // 2

    def rows(z, y):
        first, second = (
            jnp.broadcast_to(pad[f, z, pl.ds(y, 1), :], (ROWS, width)) for f in range(2)
        )
        return jnp.where(of_field, first, second)

    def state_of(peer):
        pieces = []
        for c in range(CAP):
            number = asked[peer, 0, CAP * me + c]
            z = lax.div(number, lateral) + 1
            y = lax.rem(number, lateral) + EDGE
            centre = rows(z, y)
            upper = jnp.where(part == 1, rows(z + 1, y), rows(z, y + 1))
            lower = jnp.where(part == 1, rows(z - 1, y), rows(z, y - 1))
            upper = jnp.where(part == 3, pltpu.roll(centre, width - 1, 1), upper)
            lower = jnp.where(part == 3, pltpu.roll(centre, 1, 1), lower)
            slope = limited(centre, upper, lower)
            slope = jnp.where((part < 3) | x_inside, slope, 0.0)
            pieces.append(jnp.where(part == 0, centre, slope))
        return jnp.concatenate(pieces, axis=0).astype(jnp.bfloat16)

    def answer_step(step, carry):
        peer = other(step)
        ask(peer, peer).wait_recv()
        sending[peer] = state_of(peer)
        answer(peer, me).start()
        return carry

    lax.fori_loop(0, n_tile - 1, answer_step, 0)
    states[me] = state_of(me)

    load_weights.wait()
    kind = lax.broadcasted_iota(jnp.int32, (CAP * ROWS, width), 0) // 2

    def sum_over(source):
        state = states[source]
        zero = jnp.zeros_like(state)
        left = jnp.concatenate(
            [jnp.where(kind == i, state, zero) for i in range(CAP * 4)], axis=1
        )
        right = jnp.concatenate(
            [weights[0, CAP * source + i // 4, i % 4] for i in range(CAP * 4)], axis=1
        )
        first = pl.multiple_of(source * (CAP * ROWS), CAP * ROWS)
        partial[pl.ds(first, CAP * ROWS), :] = against(left, right)

    def sum_step(step, carry):
        source = other(step)
        answer(source, source).wait_recv()
        sum_over(source)
        return carry

    sum_over(me)
    lax.fori_loop(0, n_tile - 1, sum_step, 0)

    total = partial[...]
    high = total.astype(jnp.bfloat16)
    low = (total - high.astype(jnp.float32)).astype(jnp.bfloat16)
    summed = jnp.dot(one_hot, high, preferred_element_type=jnp.float32) + jnp.dot(
        one_hot, low, preferred_element_type=jnp.float32
    )
    out[...] = summed / volume_2[...]

    for sends, _, copy in halos:
        pl.when(sends)(copy.wait_send)

    def finish(step, carry):
        peer = other(step)
        ask(peer, me).wait_send()
        answer(peer, me).wait_send()
        return carry

    lax.fori_loop(0, n_tile - 1, finish, 0)


def per_device(n_depth, n_tile, old_fields, recv_block, recv_count, new_block, moments, new_volume):
    fields, layers, lateral, width = old_fields.shape
    slots = recv_block.shape[1]
    new_count = new_volume.shape[1]
    anywhere = pl.BlockSpec(memory_space=pltpu.HBM)
    result = pl.pallas_call(
        functools.partial(kernel, n_depth, n_tile),
        out_shape=pltpu.VMEM((2 * new_count, width), jnp.float32),
        in_specs=[anywhere] * 6,
        out_specs=pl.BlockSpec(memory_space=pltpu.VMEM),
        scratch_shapes=[
            pltpu.VMEM((fields, layers + 2, lateral + 2 * EDGE, width), jnp.float32),
            pltpu.VMEM((2, fields, layers, width), jnp.float32),
            pltpu.VMEM((2, fields, layers, width), jnp.float32),
            pltpu.SMEM((n_tile, 1, slots), jnp.int32),
            pltpu.VMEM(moments.shape, jnp.bfloat16),
            pltpu.SMEM(recv_count.shape, jnp.int32),
            pltpu.SMEM(new_block.shape, jnp.int32),
            pltpu.VMEM(new_volume.shape, jnp.float32),
            pltpu.VMEM((2 * new_count, width), jnp.float32),
            pltpu.VMEM((slots * ROWS, width), jnp.float32),
            pltpu.VMEM((n_tile, CAP * ROWS, width), jnp.bfloat16),
            pltpu.VMEM((n_tile, CAP * ROWS, width), jnp.bfloat16),
            pltpu.SemaphoreType.DMA((6,)),
            pltpu.SemaphoreType.DMA((n_tile,)),
            pltpu.SemaphoreType.DMA((n_tile,)),
            pltpu.SemaphoreType.DMA((4,)),
            pltpu.SemaphoreType.DMA((4,)),
            pltpu.SemaphoreType.DMA((n_tile,)),
            pltpu.SemaphoreType.DMA((n_tile,)),
        ],
        compiler_params=pltpu.CompilerParams(
            collective_id=0, has_side_effects=True, vmem_limit_bytes=56 * 2**20
        ),
    )(old_fields, recv_block, recv_count, new_block, moments, new_volume)
    return result.reshape(1, new_count, 2, width)


def solution(mesh):
    placed = (
        P(None, "depth", "tile", None),
        P("depth", "tile"),
        P("depth", "tile"),
        P("depth", "tile"),
        P("depth", "tile", None, None, None),
        P("depth", "tile", None),
    )
    return jax.shard_map(
        functools.partial(per_device, mesh.shape["depth"], mesh.shape["tile"]),
        mesh=mesh,
        in_specs=placed,
        out_specs=P("depth", "tile", None, None),
        check_vma=False,
    )
```

time: 18.3 us -> 16 us (0.87)
  other arithmetic: 1.63 us -> 0 us
  Pallas kernels: 16.5 us -> 15.2 us
  local copies, waits for them, and re-layouts: 0.01 us -> 0.66 us
    div x1 -> x0, other arithmetic: 1.63 us -> none  [per_device(): result = summed.reshape(new_count, 2, width) / new_volume[0][:, None, :]]
    pallas_call x1, Pallas kernels: 16.5 us -> 15.2 us  [per_device(): pl.pallas_call(functools.partial(kernel, n_depth, n_tile), out_shape=pltp...]
    unnamed x2 -> x1, local copies, waits for them, and re-layouts: 0.01 us -> 0.66 us
where the time goes in v2:
time: 16 us; the launch traced here: 15.8 us
  Pallas kernels  15.2 us (95%)
  local copies, waits for them, and re-layouts  0.66 us (4%)
    pallas_call x1, Pallas kernels, per_device(): pl.pallas_call(functools.partial(kernel, n_depth, n_tile), out_shape=pltp...  15.2 us
    unnamed x1, local copies, waits for them, and re-layouts  0.66 us

profile of v2, /device:TPU:0, one launch (start us, length us, event | category | flops | bytes accessed | tf_op | source)
XLA Modules:
  0.0 15.8 jit_solution(6455274724597950419)
XLA Ops:
  0.0 15.2 %shard_map.64 = f32[256,128]{1,0:T(8,128)S(1)} custom-call(f32[2,8,64,128]{3,2,1,0:T(8,128)} %fields.1, s32[1,16]{1,0:T(1,128)} %blocks.1, s32[1,8]{1,0:T(1,128)} %counts.1, s32[1,16]{1,0:T(1,128)} %targets.1, bf16[1,16,4,128,128]{4,3,2,1,0:T(8,128)(2,1)} %moments.1, f32[1,128,128]{2,1,0:T(8,128)} %volume.1), custom_call_target="tpu_custom_call" | custom-call | tf_op jit(solution)/shard_map/pallas_call | solution.py:268
  15.2 0.7 %copy.8 = f32[1,128,2,128]{3,2,1,0:T(2,128)} copy(f32[1,128,2,128]{3,2,1,0:T(2,128)S(1)} %bitcast.1) | data formatting | bytes 262144

commit v3 on v2

--- a/solution.py
+++ b/solution.py
@@ -72,14 +72,9 @@
 
     load_asked.start()
     load_fields.start()
-    load_weights.start()
     load_count.start()
     load_target.start()
     load_volume.start()
-
-    load_fields.wait()
-    ends[0] = pad[:, body, EDGE, :]
-    ends[1] = pad[:, body, EDGE + lateral - 1, :]
 
     edges = (depth > 0).astype(jnp.int32) + (depth < n_depth - 1).astype(jnp.int32)
     pl.semaphore_wait(barrier, n_tile - 1 + edges)
@@ -125,8 +120,12 @@
         return carry
 
     lax.fori_loop(0, n_tile - 1, ask_step, 0)
+    load_fields.wait()
+    ends[0] = pad[:, body, EDGE, :]
+    ends[1] = pad[:, body, EDGE + lateral - 1, :]
     for sends, _, copy in halos:
         pl.when(sends)(copy.start)
+    load_weights.start()
 
     load_count.wait()
     load_target.wait()
@@ -243,8 +242,10 @@
     total = partial[...]
     high = total.astype(jnp.bfloat16)
     low = (total - high.astype(jnp.float32)).astype(jnp.bfloat16)
-    summed = jnp.dot(one_hot, high, preferred_element_type=jnp.float32) + jnp.dot(
-        one_hot, low, preferred_element_type=jnp.float32
+    summed = jnp.dot(
+        jnp.concatenate([one_hot, one_hot], axis=1),
+        jnp.concatenate([high, low], axis=0),
+        preferred_element_type=jnp.float32,
     )
     out[...] = summed / volume_2[...]
 

time: 16 us -> 16 us (level)
  no operation moved by 1% of the time
where the time goes in v3:
time: 16 us; the launch traced here: 15.8 us
  Pallas kernels  15.2 us (95%)
  local copies, waits for them, and re-layouts  0.66 us (4%)
    pallas_call x1, Pallas kernels, per_device(): pl.pallas_call(functools.partial(kernel, n_depth, n_tile), out_shape=pltp...  15.2 us
    unnamed x1, local copies, waits for them, and re-layouts  0.66 us

profile of v3, /device:TPU:0, one launch (start us, length us, event | category | flops | bytes accessed | tf_op | source)
XLA Modules:
  0.0 15.8 jit_solution(11683936269774492118)
XLA Ops:
  0.0 15.2 %shard_map.64 = f32[256,128]{1,0:T(8,128)S(1)} custom-call(f32[2,8,64,128]{3,2,1,0:T(8,128)} %fields.1, s32[1,16]{1,0:T(1,128)} %blocks.1, s32[1,8]{1,0:T(1,128)} %counts.1, s32[1,16]{1,0:T(1,128)} %targets.1, bf16[1,16,4,128,128]{4,3,2,1,0:T(8,128)(2,1)} %moments.1, f32[1,128,128]{2,1,0:T(8,128)} %volume.1), custom_call_target="tpu_custom_call" | custom-call | tf_op jit(solution)/shard_map/pallas_call | solution.py:269
  15.2 0.7 %copy.8 = f32[1,128,2,128]{3,2,1,0:T(2,128)} copy(f32[1,128,2,128]{3,2,1,0:T(2,128)S(1)} %bitcast.1) | data formatting | bytes 262144
